TPU v7x, 256 devices: a whole 4x4x8 slice. The times are simulated.
256 devices in a mesh: rcv: 256 (over x, z, y, core).
Axes of the slice: x: 4, y: 4, z: 8, core: 2. Of those that a mesh axis runs over, the one named last changes fastest.
Arguments:
- predictions: bfloat16 [262144, 384], P('rcv'), may hold values from -6 to 6
- observed: bfloat16 [2, 262144, 1024], P(None, 'rcv'), may hold values from -0.3984375 to 0.3984375
- partners: int32 [2, 256], replicated, may hold values from 0 to 255, as said below
- green_block: bfloat16 [262144, 512], P('rcv'), may hold values from -0.046875 to 0.046875
Outputs:
- gradient: float32 [512, 384], P('rcv')
Inputs may be any that keep to these rules, and one draw needn't show every extreme that they name: `partners`: row m pairs block b with block b XOR s_m for a meeting offset s_m; s_0 lies in 1 to 254 and s_1 = s_0 XOR (255).
All inputs are finite; a program needn't handle non-finite values.
Results may differ from a plain program's by a relative error of at most 0.0034.
Values may be sent and summed in bfloat16 or wider, within the bound.
A program may use at most 64 MiB of HBM per device.

v0:
```python
import functools

import jax
import jax.numpy as jnp
import numpy as np
from jax import lax
from jax.experimental import pallas as pl
from jax.experimental.pallas import tpu as pltpu
from jax.sharding import PartitionSpec as P

STUDENT_NU = 0.01
MESH = pl.DeviceIdType.MESH
CHUNK = 128
ROWS = 512
CORE_BITS, Y_BITS, Z_BITS, X_BITS = 1, 2, 3, 2
STATIC = ("core", "x1", "y1", "x3", "y3")
LAGS = (0, 1, 2, 3, 4, 5, 6, 7, 8, 9, 10, 11, 12, 13)


def flipped(index, mask):
    return lax.bitwise_xor(index, jnp.int32(mask))


def remote(src, dst, send, recv, target):
    return pltpu.make_async_remote_copy(
        src_ref=src, dst_ref=dst, send_sem=send, recv_sem=recv, device_id=(target,), device_id_type=MESH
    )


def greet(peers):
    barrier = pltpu.get_barrier_semaphore()
    for peer in peers:
        pl.semaphore_signal(barrier, inc=1, device_id=(peer,), device_id_type=MESH)
    pl.semaphore_wait(barrier, len(peers))


def cell_order(row):
    pair = row & 1
    z = (row >> 1) & (2**Z_BITS - 1)
    x = (row >> (1 + Z_BITS)) & (2**X_BITS - 1)
    y = (row >> (1 + Z_BITS + X_BITS)) & (2**Y_BITS - 1)
    core = row >> (1 + Z_BITS + X_BITS + Y_BITS)
    device = (((x << Z_BITS) + z << Y_BITS) + y << CORE_BITS) + core
    return device * 2 + pair


def tile_kernel(direct, spec, flag_ref, p_ref, o_hbm, g_hbm, order_hbm, grad_ref, o_ref, g_ref, order_ref, gt_ref, weights, theirs, answers, own, *rest):
    levels, full = spec["levels"], spec["full"]
    names, lags = spec["names"], spec["lags"]
    buffers = dict(zip(names, rest[: len(names)]))
    rest = rest[len(names) :]
    o_sem, g_sem, order_sem = rest[:3]
    sends = rest[3::2]
    receives = rest[4::2]
    me = lax.axis_index("rcv")
    rows, samples = p_ref.shape
    count = rows // CHUNK
    inverse = 1.0 / samples
    peers = [flipped(me, mask) for mask in levels]
    if direct:
        peers.append(flipped(me, direct))
    peers.append(flipped(me, full))

    def part(j):
        return pl.ds(pl.multiple_of(j * CHUNK, CHUNK), CHUNK)

    def copy(k, mask, src, dst):
        return lambda j: remote(
            src.at[part(j)], dst.at[part(j)], sends[k].at[j], receives[k].at[j], flipped(me, mask)
        )

    depth = len(levels)
    held = [p_ref] + [buffers[f"kept{k}"] for k in range(depth)]
    if not direct:
        held[depth] = theirs.at[0]
    out_copies = [copy(k, levels[k], held[k], buffers[f"got{k}"]) for k in range(depth)]
    near, far = theirs.at[0], theirs.at[1]
    v_near, v_far = answers.at[0], answers.at[1]
    back, total = buffers["back"], buffers["total"]
    go_near = copy(depth, direct, held[depth], near) if direct else None
    go_far = copy(depth + 1, full, near, far)
    go_back = copy(depth + 2, full, v_far, back)
    home = buffers["home"] if direct else total
    go_home = copy(depth + 3, direct, total, home) if direct else None
    returned = [home] + [buffers[f"sum{k}"] for k in range(depth)]
    home_copies = [
        copy(depth + 4 + k, levels[depth - 1 - k], returned[k], buffers[f"ret{k}"]) for k in range(depth)
    ]

    o_copy = pltpu.make_async_copy(o_hbm, o_ref, o_sem)
    g_copy = pltpu.make_async_copy(g_hbm, g_ref, g_sem)
    order_copy = pltpu.make_async_copy(order_hbm, order_ref, order_sem)
    o_copy.start()
    g_copy.start()
    order_copy.start()
    greet(peers)

    first_copy = out_copies[0] if depth else go_near

    @pl.loop(0, count)
    def _(j):
        first_copy(j).start()

    o_copy.wait()
    g_copy.wait()
    order_copy.wait()

    @pl.loop(0, rows // ROWS)
    def _(j):
        lines = pl.ds(pl.multiple_of(j * ROWS, ROWS), ROWS)
        gt_ref[:, lines] = lax.dot_general(
            order_ref[...], g_ref[lines], (((1,), (1,)), ((), ())), preferred_element_type=jnp.float32
        ).astype(jnp.bfloat16)

    first = flag_ref[0]

    def choose(k, got, kept, j):
        picked = jnp.broadcast_to(flag_ref[1 + k] == 1, (CHUNK, samples))
        return jnp.where(
            picked, got[part(j)].astype(jnp.float32), kept[part(j)].astype(jnp.float32)
        ).astype(jnp.bfloat16)

    def tile(j, side):
        rows_in = theirs[side, part(j)]
        which = first ^ side

        def block(i, acc):
            lines = pl.ds(pl.multiple_of(i * ROWS, ROWS), ROWS)
            mine = p_ref[lines]
            gram = lax.dot_general(mine, rows_in, (((1,), (1,)), ((), ())), preferred_element_type=jnp.float32)
            residual = gram * inverse - o_ref[which, lines, part(j)].astype(jnp.float32)
            weight = ((STUDENT_NU + 1.0) * residual / (STUDENT_NU + residual * residual)).astype(jnp.bfloat16)
            weights[side, lines, part(j)] = weight
            return acc + lax.dot_general(weight, mine, (((0,), (0,)), ((), ())), preferred_element_type=jnp.float32)

        acc = lax.fori_loop(0, rows // ROWS, block, jnp.zeros((CHUNK, samples), jnp.float32))
        answers[side, part(j)] = (acc * inverse).astype(jnp.bfloat16)

    def level_step(k):
        def run(j):
            out_copies[k](j).wait_recv()
            held[k + 1][part(j)] = choose(k, buffers[f"got{k}"], held[k], j)
            after = out_copies[k + 1] if k + 1 < depth else (go_near if direct else go_far)
            after(j).start()

        return run

    def tile_steps(t, lag_near, lag_far):
        @pl.loop(0, 2)
        def _(side):
            j = t - lag_near - side * (lag_far - lag_near)

            @pl.when((j >= 0) & (j < count))
            def _():
                @pl.when(side == 0)
                def _():
                    if direct:
                        go_near(j).wait_recv()
                        go_far(j).start()

                @pl.when(side == 1)
                def _():
                    go_far(j).wait_recv()

                tile(j, side)

                @pl.when(side == 1)
                def _():
                    go_back(j).start()

    def back_step(j):
        go_back(j).wait_recv()
        total[part(j)] = (
            v_near[part(j)].astype(jnp.float32) + back[part(j)].astype(jnp.float32)
        ).astype(jnp.bfloat16)
        if direct:
            go_home(j).start()
        elif depth:
            home_copies[0](j).start()

    def home_step(j):
        go_home(j).wait_recv()
        if depth:
            home_copies[0](j).start()

    def return_step(k):
        def run(j):
            home_copies[k](j).wait_recv()
            returned[k + 1][part(j)] = choose(depth - 1 - k, buffers[f"ret{k}"], returned[k], j)
            if k + 1 < depth:
                home_copies[k + 1](j).start()

        return run

    def own_step(j):
        own[part(j)] = jnp.dot(weights[0, part(j)], theirs[0], preferred_element_type=jnp.float32) + jnp.dot(
            weights[1, part(j)], theirs[1], preferred_element_type=jnp.float32
        )

    steps = [level_step(k) for k in range(depth)] + ["near", "far", back_step]
    steps += [home_step] if direct else [None]
    steps += [return_step(k) for k in range(depth)]
    when = list(lags[: len(steps)])
    own_lag = when[depth + 1] + count
    assert all(a is not None for a in when)

    @pl.loop(0, count + max(max(when), own_lag))
    def _(t):
        for step, lag in zip(steps, when):
            if step == "near":
                tile_steps(t, lag, when[depth + 1])
            elif step not in (None, "far"):

                @pl.when((t >= lag) & (t < lag + count))
                def _(step=step, lag=lag):
                    step(t - lag)

        @pl.when(t >= own_lag)
        def _():
            @pl.when(t < own_lag + count)
            def _():
                own_step(t - own_lag)

    last = returned[depth]
    grad_ref[...] = jnp.zeros_like(grad_ref)

    @pl.loop(0, rows // 256)
    def _(j):
        lines = pl.ds(pl.multiple_of(j * 256, 256), 256)
        adjoint = (own[lines] * inverse + last[lines].astype(jnp.float32)).astype(jnp.bfloat16)
        grad_ref[...] += jnp.dot(gt_ref[:, lines], adjoint, preferred_element_type=jnp.float32)

    started = out_copies + ([go_near] if direct else []) + [go_far, go_back]
    started += ([go_home] if direct else []) + home_copies

    @pl.loop(0, count)
    def _(j):
        for one in started:
            one(j).wait_send()


def tile_call(direct, spec, identity, flags, predictions, observed, green, order):
    rows, samples = predictions.shape
    count = rows // CHUNK
    cells = green.shape[1]
    depth = len(spec["levels"])
    block = pltpu.VMEM((rows, samples), jnp.bfloat16)
    sems = pltpu.SemaphoreType.DMA((count,))
    anywhere = pl.BlockSpec(memory_space=pl.ANY)
    return pl.pallas_call(
        functools.partial(tile_kernel, direct, spec),
        out_shape=jax.ShapeDtypeStruct((cells, samples), jnp.float32),
        in_specs=[
            pl.BlockSpec(memory_space=pltpu.SMEM),
            pl.BlockSpec(memory_space=pltpu.VMEM),
            anywhere, anywhere, anywhere,
        ],
        out_specs=pl.BlockSpec(memory_space=pltpu.VMEM),
        scratch_shapes=[
            pltpu.VMEM(observed.shape, jnp.bfloat16),
            pltpu.VMEM(green.shape, jnp.bfloat16),
            pltpu.VMEM(order.shape, jnp.bfloat16),
            pltpu.VMEM((cells, rows), jnp.bfloat16),
            pltpu.VMEM((2, rows, rows), jnp.bfloat16),
            pltpu.VMEM((2, rows, samples), jnp.bfloat16),
            pltpu.VMEM((2, rows, samples), jnp.bfloat16),
            pltpu.VMEM((rows, samples), jnp.float32),
            *[block] * len(spec["names"]),
            *[pltpu.SemaphoreType.DMA] * 3,
            *[sems] * (2 * (4 + 2 * depth)),
        ],
        compiler_params=pltpu.CompilerParams(
            collective_id=1 + identity, has_side_effects=True, vmem_limit_bytes=44 * 2**20
        ),
        name=f"tiles_{direct}",
    )(flags, predictions, observed, green, order)


def sum_kernel(part_ref, out_ref, got_core, held, got_plane, piece, got_line, sc, rc, sp, rp, sl, rl):
    me = lax.axis_index("rcv")
    core = me & 1
    y = (me >> CORE_BITS) & (2**Y_BITS - 1)
    z = (me >> (CORE_BITS + Y_BITS)) & (2**Z_BITS - 1)
    x = me >> (CORE_BITS + Y_BITS + Z_BITS)
    plane = 2 ** (X_BITS + Y_BITS)
    line = 2**Z_BITS
    spot = y * 2**X_BITS + x

    def plane_mask(k):
        kx, ky = k % 2**X_BITS, k // 2**X_BITS
        return (kx << (CORE_BITS + Y_BITS + Z_BITS)) | (ky << CORE_BITS)

    def line_mask(k):
        return k << (CORE_BITS + Y_BITS)

    twin = flipped(me, 1)
    planes = [flipped(me, plane_mask(k)) for k in range(1, plane)]
    lines = [flipped(me, line_mask(k)) for k in range(1, line)]
    greet([twin] + planes + lines)

    across = remote(part_ref.at[1 - core], got_core, sc, rc, twin)
    across.start()
    across.wait_recv()
    held[...] = part_ref[core] + got_core[...]
    copies = []
    for k in range(1, plane):
        copy = remote(
            held.at[flipped(spot, k)], got_plane.at[k - 1], sp.at[k - 1], rp.at[k - 1], planes[k - 1]
        )
        copy.start()
        copies.append(copy)
    total = held[spot]
    for k in range(1, plane):
        copies[k - 1].wait_recv()
        total = total + got_plane[k - 1]
    for k in range(line):
        piece[k] = total[2 * k : 2 * k + 2]
    for k in range(1, line):
        copy = remote(
            piece.at[flipped(z, k)], got_line.at[k - 1], sl.at[k - 1], rl.at[k - 1], lines[k - 1]
        )
        copy.start()
        copies.append(copy)
    result = piece[z]
    for k in range(1, line):
        copies[plane - 2 + k].wait_recv()
        result = result + got_line[k - 1]
    out_ref[...] = result
    across.wait_send()
    for copy in copies:
        copy.wait_send()


def sum_call(part):
    cells, samples = part.shape
    plane = 2 ** (X_BITS + Y_BITS)
    line = 2**Z_BITS
    lot = cells // (2 * plane)
    dma = pltpu.SemaphoreType.DMA
    return pl.pallas_call(
        sum_kernel,
        out_shape=jax.ShapeDtypeStruct((2, samples), jnp.float32),
        in_specs=[pl.BlockSpec(memory_space=pltpu.VMEM)],
        out_specs=pl.BlockSpec(memory_space=pltpu.VMEM),
        scratch_shapes=[
            pltpu.VMEM((plane, lot, samples), jnp.float32),
            pltpu.VMEM((plane, lot, samples), jnp.float32),
            pltpu.VMEM((plane - 1, lot, samples), jnp.float32),
            pltpu.VMEM((line, 2, samples), jnp.float32),
            pltpu.VMEM((line - 1, 2, samples), jnp.float32),
            dma, dma, dma((plane - 1,)), dma((plane - 1,)), dma((line - 1,)), dma((line - 1,)),
        ],
        compiler_params=pltpu.CompilerParams(collective_id=0, has_side_effects=True),
        name="sum_cells",
    )(part.reshape(2, plane, lot, samples))


def bit(value, place):
    return lax.shift_right_logical(value, jnp.int32(place)) & 1


def layout():
    y, z, x = CORE_BITS, CORE_BITS + Y_BITS, CORE_BITS + Y_BITS + Z_BITS
    return y, z, x


def shards(predictions, observed, partners, green_block):
    devices = lax.axis_size("rcv")
    full = devices - 1
    y, z, x = layout()
    offset = partners[0, 0]
    swapped = bit(offset, x - 1)
    near = jnp.where(swapped == 1, lax.bitwise_xor(offset, full), offset)
    steps = dict(
        core=(bit(near, 0), 1),
        x1=(bit(near, x) ^ bit(near, x + 1), 1 << x),
        y1=(bit(near, y) ^ bit(near, y + 1), 1 << y),
        x3=(bit(near, x + 1), 3 << x),
        y3=(bit(near, y + 1), 3 << y),
    )
    levels = [steps[name][1] for name in STATIC]
    flags = jnp.stack([swapped] + [steps[name][0] for name in STATIC]).astype(jnp.int32)
    fields = [(bit(near, z + k), 1 << (z + k)) for k in range(Z_BITS - 1)]
    fields += [steps[name] for name in steps if name not in STATIC]
    directs = [0]
    which = jnp.int32(0)
    for k, (value, mask) in enumerate(fields):
        directs = directs + [one ^ mask for one in directs]
        which = which + (value << k)
    depth = len(levels)
    names = [f"got{k}" for k in range(depth)] + [f"kept{k}" for k in range(depth)]
    names += ["back", "total", "home"]
    names += [f"ret{k}" for k in range(depth)] + [f"sum{k}" for k in range(depth)]
    spec = dict(levels=levels, full=full, names=names, lags=LAGS)
    cells = green_block.shape[1]
    order = np.zeros((cells, cells), np.float32)
    order[np.arange(cells), cell_order(np.arange(cells))] = 1.0
    calls = [functools.partial(tile_call, direct, spec, k) for k, direct in enumerate(directs)]
    operands = (flags, predictions, observed, green_block, jnp.asarray(order, jnp.bfloat16))
    part = lax.switch(which, calls, *operands) if len(calls) > 1 else calls[0](*operands)
    return sum_call(part)


def solution(mesh):
    placed = (P("rcv", None), P(None, "rcv", None), P(), P("rcv", None))
    return jax.shard_map(
        shards, mesh=mesh, in_specs=placed, out_specs=P("rcv", None), check_vma=False
    )
```

profile of v0, /device:TPU:2, one launch (start us, length us, event | category | flops | bytes accessed | tf_op | source)
XLA Modules:
  0.0 160.0 jit_solution(7277613308127868300)
XLA Ops:
  0.0 1.2 slice.3
  3.1 0.1 stack.27
  3.2 133.1 %conditional.1 = (f32[512,384]{1,0:T(8,128)S(1)}) conditional(s32[]{:T(128)} %clamp.3, (s32[6]{0:T(128)S(1)}, bf16[1024,384]{1,0:T(8,128)(2,1)}, bf16[2,1024,1024]{2,1,0:T(8,128)(2,1)}, bf16[1024,512]{1,0:T(8,128)(2,1)}, bf16[512,512]{1,0:T(8,128)(2,1)}) %tuple.17, (s32[6]{0:T(128)S(1)}, bf16[1024,384]{1,0:T(8,128)(2,1)}, ...), branch_computations={%region_0.1_spmd, %region_1.2_spmd, %region_2.3_spmd, %region_3.4_... | conditional | bytes 8 | solution.py:400
  3.2 133.1 %tiles_24.1 = f32[512,384]{1,0:T(8,128)S(1)} custom-call(s32[6]{0:T(128)S(1)} %get-tuple-element.65.flag_ref, bf16[1024,384]{1,0:T(8,128)(2,1)} %get-tuple-element.66.p_ref, bf16[2,1024,1024]{2,1,0:T(8,128)(2,1)} %get-tuple-element.67.o_hbm, bf16[1024,512]{1,0:T(8,128)(2,1)} %get-tuple-element.68.g_hbm, bf16[512,512]{1,0:T(8,128)(2,1)} %get-tuple-element.69.order_hbm), custom_call_target="tpu_custom_call" | custom-call | tf_op jit(solution)/shard_map/cond/branch_3_fun/tiles_24/pallas_call | solution.py:250
  136.3 22.4 %sum_cells.1 = f32[2,384]{1,0:T(2,128)} custom-call(f32[2,16,16,384]{3,2,1,0:T(8,128)S(1)} %bitcast.8), custom_call_target="tpu_custom_call" | custom-call | tf_op jit(solution)/shard_map/sum_cells/pallas_call | solution.py:340
  158.8 1.2 copy.11
where the time goes:
time: 160 us
  Pallas kernels  156 us (98%)
  local copies, waits for them, and re-layouts  2.51 us (2%)
  between operations  1.97 us (1%)
    pallas_call x1, Pallas kernels, tile_call(): pl.pallas_call(functools.partial(tile_kernel, direct, spec), out_shape=ja...  133 us
    pallas_call x1, Pallas kernels, sum_call(): pl.pallas_call(sum_kernel, out_shape=jax.ShapeDtypeStruct((2, samples), j...  22.4 us

commit v1 on v0

--- a/solution.py
+++ b/solution.py
@@ -11,10 +11,10 @@
 STUDENT_NU = 0.01
 MESH = pl.DeviceIdType.MESH
 CHUNK = 128
-ROWS = 512
+ROWS = 256
 CORE_BITS, Y_BITS, Z_BITS, X_BITS = 1, 2, 3, 2
-STATIC = ("core", "x1", "y1", "x3", "y3")
-LAGS = (0, 1, 2, 3, 4, 5, 6, 7, 8, 9, 10, 11, 12, 13)
+STATIC = ("core", "x1", "y1")
+LAGS = (0, 1, 2, 3, 4, 5, 6, 7, 8, 9)
 
 
 def flipped(index, mask):
@@ -44,14 +44,14 @@
     return device * 2 + pair
 
 
-def tile_kernel(direct, spec, flag_ref, p_ref, o_hbm, g_hbm, order_hbm, grad_ref, o_ref, g_ref, order_ref, gt_ref, weights, theirs, answers, own, *rest):
+def tile_kernel(direct, spec, flag_ref, p_ref, o_hbm, adjoint_ref, o_ref, weights, theirs, answers, own, *rest):
     levels, full = spec["levels"], spec["full"]
     names, lags = spec["names"], spec["lags"]
     buffers = dict(zip(names, rest[: len(names)]))
     rest = rest[len(names) :]
-    o_sem, g_sem, order_sem = rest[:3]
-    sends = rest[3::2]
-    receives = rest[4::2]
+    o_sem = rest[0]
+    sends = rest[1::2]
+    receives = rest[2::2]
     me = lax.axis_index("rcv")
     rows, samples = p_ref.shape
     count = rows // CHUNK
@@ -88,11 +88,7 @@
     ]
 
     o_copy = pltpu.make_async_copy(o_hbm, o_ref, o_sem)
-    g_copy = pltpu.make_async_copy(g_hbm, g_ref, g_sem)
-    order_copy = pltpu.make_async_copy(order_hbm, order_ref, order_sem)
     o_copy.start()
-    g_copy.start()
-    order_copy.start()
     greet(peers)
 
     first_copy = out_copies[0] if depth else go_near
@@ -102,16 +98,6 @@
         first_copy(j).start()
 
     o_copy.wait()
-    g_copy.wait()
-    order_copy.wait()
-
-    @pl.loop(0, rows // ROWS)
-    def _(j):
-        lines = pl.ds(pl.multiple_of(j * ROWS, ROWS), ROWS)
-        gt_ref[:, lines] = lax.dot_general(
-            order_ref[...], g_ref[lines], (((1,), (1,)), ((), ())), preferred_element_type=jnp.float32
-        ).astype(jnp.bfloat16)
-
     first = flag_ref[0]
 
     def choose(k, got, kept, j):
@@ -222,13 +208,7 @@
                 own_step(t - own_lag)
 
     last = returned[depth]
-    grad_ref[...] = jnp.zeros_like(grad_ref)
-
-    @pl.loop(0, rows // 256)
-    def _(j):
-        lines = pl.ds(pl.multiple_of(j * 256, 256), 256)
-        adjoint = (own[lines] * inverse + last[lines].astype(jnp.float32)).astype(jnp.bfloat16)
-        grad_ref[...] += jnp.dot(gt_ref[:, lines], adjoint, preferred_element_type=jnp.float32)
+    adjoint_ref[...] = (own[...] * inverse + last[...].astype(jnp.float32)).astype(jnp.bfloat16)
 
     started = out_copies + ([go_near] if direct else []) + [go_far, go_back]
     started += ([go_home] if direct else []) + home_copies
@@ -239,44 +219,40 @@
             one(j).wait_send()
 
 
-def tile_call(direct, spec, identity, flags, predictions, observed, green, order):
+def tile_call(direct, spec, identity, flags, predictions, observed):
     rows, samples = predictions.shape
     count = rows // CHUNK
-    cells = green.shape[1]
     depth = len(spec["levels"])
     block = pltpu.VMEM((rows, samples), jnp.bfloat16)
     sems = pltpu.SemaphoreType.DMA((count,))
     anywhere = pl.BlockSpec(memory_space=pl.ANY)
     return pl.pallas_call(
         functools.partial(tile_kernel, direct, spec),
-        out_shape=jax.ShapeDtypeStruct((cells, samples), jnp.float32),
+        out_shape=jax.ShapeDtypeStruct((rows, samples), jnp.bfloat16),
         in_specs=[
             pl.BlockSpec(memory_space=pltpu.SMEM),
             pl.BlockSpec(memory_space=pltpu.VMEM),
-            anywhere, anywhere, anywhere,
+            anywhere,
         ],
         out_specs=pl.BlockSpec(memory_space=pltpu.VMEM),
         scratch_shapes=[
             pltpu.VMEM(observed.shape, jnp.bfloat16),
-            pltpu.VMEM(green.shape, jnp.bfloat16),
-            pltpu.VMEM(order.shape, jnp.bfloat16),
-            pltpu.VMEM((cells, rows), jnp.bfloat16),
             pltpu.VMEM((2, rows, rows), jnp.bfloat16),
             pltpu.VMEM((2, rows, samples), jnp.bfloat16),
             pltpu.VMEM((2, rows, samples), jnp.bfloat16),
             pltpu.VMEM((rows, samples), jnp.float32),
             *[block] * len(spec["names"]),
-            *[pltpu.SemaphoreType.DMA] * 3,
+            pltpu.SemaphoreType.DMA,
             *[sems] * (2 * (4 + 2 * depth)),
         ],
         compiler_params=pltpu.CompilerParams(
             collective_id=1 + identity, has_side_effects=True, vmem_limit_bytes=44 * 2**20
         ),
         name=f"tiles_{direct}",
-    )(flags, predictions, observed, green, order)
-
-
-def sum_kernel(part_ref, out_ref, got_core, held, got_plane, piece, got_line, sc, rc, sp, rp, sl, rl):
+    )(flags, predictions, observed)
+
+
+def sum_kernel(adjoint_ref, g_ref, order_ref, out_ref, gt_ref, part, got_core, held, got_plane, piece, got_line, sc, rc, sp, rp, sl, rl):
     me = lax.axis_index("rcv")
     core = me & 1
     y = (me >> CORE_BITS) & (2**Y_BITS - 1)
@@ -296,20 +272,47 @@
     twin = flipped(me, 1)
     planes = [flipped(me, plane_mask(k)) for k in range(1, plane)]
     lines = [flipped(me, line_mask(k)) for k in range(1, line)]
-    greet([twin] + planes + lines)
-
-    across = remote(part_ref.at[1 - core], got_core, sc, rc, twin)
-    across.start()
+    peers = [twin] + planes + lines
+    barrier = pltpu.get_barrier_semaphore()
+    for peer in peers:
+        pl.semaphore_signal(barrier, inc=1, device_id=(peer,), device_id_type=MESH)
+
+    half = got_core.shape[0]
+    lot = half // plane
+
+    @pl.loop(0, g_ref.shape[0] // ROWS)
+    def _(j):
+        lines_in = pl.ds(pl.multiple_of(j * ROWS, ROWS), ROWS)
+        gt_ref[:, lines_in] = lax.dot_general(
+            order_ref[...], g_ref[lines_in], (((1,), (1,)), ((), ())), preferred_element_type=jnp.float32
+        ).astype(jnp.bfloat16)
+
+    @pl.loop(0, 2)
+    def _(k):
+        side = (1 - core) ^ k
+        cells = pl.ds(pl.multiple_of(side * half, half), half)
+        part[k] = jnp.dot(gt_ref[cells], adjoint_ref[...], preferred_element_type=jnp.float32)
+
+        @pl.when(k == 0)
+        def _():
+            pl.semaphore_wait(barrier, len(peers))
+            remote(part.at[0], got_core, sc, rc, twin).start()
+
+    across = remote(part.at[0], got_core, sc, rc, twin)
     across.wait_recv()
-    held[...] = part_ref[core] + got_core[...]
+    held[...] = part[1] + got_core[...]
+
+    def lot_of(index):
+        return pl.ds(pl.multiple_of(index * lot, lot), lot)
+
     copies = []
     for k in range(1, plane):
         copy = remote(
-            held.at[flipped(spot, k)], got_plane.at[k - 1], sp.at[k - 1], rp.at[k - 1], planes[k - 1]
+            held.at[lot_of(flipped(spot, k))], got_plane.at[k - 1], sp.at[k - 1], rp.at[k - 1], planes[k - 1]
         )
         copy.start()
         copies.append(copy)
-    total = held[spot]
+    total = held[lot_of(spot)]
     for k in range(1, plane):
         copies[k - 1].wait_recv()
         total = total + got_plane[k - 1]
@@ -331,28 +334,34 @@
         copy.wait_send()
 
 
-def sum_call(part):
-    cells, samples = part.shape
+def sum_call(adjoint, green, order):
+    rows, samples = adjoint.shape
+    cells = green.shape[1]
     plane = 2 ** (X_BITS + Y_BITS)
     line = 2**Z_BITS
-    lot = cells // (2 * plane)
+    half = cells // 2
+    lot = half // plane
     dma = pltpu.SemaphoreType.DMA
     return pl.pallas_call(
         sum_kernel,
         out_shape=jax.ShapeDtypeStruct((2, samples), jnp.float32),
-        in_specs=[pl.BlockSpec(memory_space=pltpu.VMEM)],
+        in_specs=[pl.BlockSpec(memory_space=pltpu.VMEM)] * 3,
         out_specs=pl.BlockSpec(memory_space=pltpu.VMEM),
         scratch_shapes=[
-            pltpu.VMEM((plane, lot, samples), jnp.float32),
-            pltpu.VMEM((plane, lot, samples), jnp.float32),
+            pltpu.VMEM((cells, rows), jnp.bfloat16),
+            pltpu.VMEM((2, half, samples), jnp.float32),
+            pltpu.VMEM((half, samples), jnp.float32),
+            pltpu.VMEM((half, samples), jnp.float32),
             pltpu.VMEM((plane - 1, lot, samples), jnp.float32),
             pltpu.VMEM((line, 2, samples), jnp.float32),
             pltpu.VMEM((line - 1, 2, samples), jnp.float32),
             dma, dma, dma((plane - 1,)), dma((plane - 1,)), dma((line - 1,)), dma((line - 1,)),
         ],
-        compiler_params=pltpu.CompilerParams(collective_id=0, has_side_effects=True),
+        compiler_params=pltpu.CompilerParams(
+            collective_id=0, has_side_effects=True, vmem_limit_bytes=20 * 2**20
+        ),
         name="sum_cells",
-    )(part.reshape(2, plane, lot, samples))
+    )(adjoint, green, order)
 
 
 def bit(value, place):
@@ -396,9 +405,9 @@
     order = np.zeros((cells, cells), np.float32)
     order[np.arange(cells), cell_order(np.arange(cells))] = 1.0
     calls = [functools.partial(tile_call, direct, spec, k) for k, direct in enumerate(directs)]
-    operands = (flags, predictions, observed, green_block, jnp.asarray(order, jnp.bfloat16))
-    part = lax.switch(which, calls, *operands) if len(calls) > 1 else calls[0](*operands)
-    return sum_call(part)
+    operands = (flags, predictions, observed)
+    adjoint = lax.switch(which, calls, *operands) if len(calls) > 1 else calls[0](*operands)
+    return sum_call(adjoint, green_block, jnp.asarray(order, jnp.bfloat16))
 
 
 def solution(mesh):

time: 160 us -> 144 us (0.900)
  Pallas kernels: 156 us -> 142 us
    pallas_call x1, Pallas kernels: 133 us -> 121 us  [tile_call(): pl.pallas_call(functools.partial(tile_kernel, direct, spec), out_shape=ja...]
where the time goes in v1:
time: 144 us; the launch traced here: 146 us
  Pallas kernels  142 us (99%)
  between operations  1.99 us (1%)
  local copies, waits for them, and re-layouts  1.78 us (1%)
    pallas_call x1, Pallas kernels, tile_call(): pl.pallas_call(functools.partial(tile_kernel, direct, spec), out_shape=ja...  121 us
    pallas_call x1, Pallas kernels, sum_call(): pl.pallas_call(sum_kernel, out_shape=jax.ShapeDtypeStruct((2, samples), j...  21 us

profile of v1, /device:TPU:2, one launch (start us, length us, event | category | flops | bytes accessed | tf_op | source)
XLA Modules:
  0.0 145.6 jit_solution(13701177288678152188)
XLA Ops:
  0.0 1.2 slice.3
  3.1 0.1 pad_add_fusion
  3.2 0.0 copy-start
  3.2 0.0 copy-start.1
  3.2 120.7 %conditional.1 = (bf16[1024,384]{1,0:T(8,128)(2,1)S(1)}) conditional(s32[]{:T(128)} %clamp.3, (s32[4]{0:T(128)S(1)}, bf16[1024,384]{1,0:T(8,128)(2,1)}, bf16[2,1024,1024]{2,1,0:T(8,128)(2,1)}) %tuple.53, (s32[4]{0:T(128)S(1)}, bf16[1024,384]{1,0:T(8,128)(2,1)}, bf16[2,1024,1024]{2,1,0:T(8,128)(2,1)}) %tuple.53, ...), branch_computations={%region_0.1_spmd, %region_1.2_spmd, %region_2.3_spmd, %region_3.4_... | conditional | bytes 8 | solution.py:409
  3.4 120.5 %tiles_198.1 = bf16[1024,384]{1,0:T(8,128)(2,1)S(1)} custom-call(s32[4]{0:T(128)S(1)} %get-tuple-element.154.flag_ref, bf16[1024,384]{1,0:T(8,128)(2,1)} %get-tuple-element.155.p_ref, bf16[2,1024,1024]{2,1,0:T(8,128)(2,1)} %get-tuple-element.156.o_hbm), custom_call_target="tpu_custom_call" | custom-call | tf_op jit(solution)/shard_map/cond/branch_12_fun/tiles_198/pallas_call | solution.py:229
  123.9 0.0 copy-done
  124.0 0.0 copy-done.1
  124.0 21.0 %sum_cells.1 = f32[2,384]{1,0:T(2,128)S(1)} custom-call(bf16[1024,384]{1,0:T(8,128)(2,1)S(1)} %get-tuple-element.166.adjoint_ref, bf16[1024,512]{1,0:T(8,128)(2,1)S(1)} %copy-done, bf16[512,512]{1,0:T(8,128)(2,1)S(1)} %copy-done.1), custom_call_target="tpu_custom_call" | custom-call | tf_op jit(solution)/shard_map/sum_cells/pallas_call | solution.py:345
  145.0 0.6 copy.23
Async XLA Ops:
  3.2 120.7 %copy-start = (bf16[1024,512]{1,0:T(8,128)(2,1)S(1)}, bf16[1024,512]{1,0:T(8,128)(2,1)}, u32[]{:S(2)}) copy-start(bf16[1024,512]{1,0:T(8,128)(2,1)} %g_ref.1) | copy-start | bytes 3145732
  3.2 120.7 %copy-start.1 = (bf16[512,512]{1,0:T(8,128)(2,1)S(1)}, bf16[512,512]{1,0:T(8,128)(2,1)}, u32[]{:S(2)}) copy-start(bf16[512,512]{1,0:T(8,128)(2,1)} %constant.22.clone.order_ref) | copy-start | bytes 1572868

commit v2 on v1

--- a/solution.py
+++ b/solution.py
@@ -11,10 +11,11 @@
 STUDENT_NU = 0.01
 MESH = pl.DeviceIdType.MESH
 CHUNK = 128
+TILE = 256
 ROWS = 256
 CORE_BITS, Y_BITS, Z_BITS, X_BITS = 1, 2, 3, 2
 STATIC = ("core", "x1", "y1")
-LAGS = (0, 1, 2, 3, 4, 5, 6, 7, 8, 9)
+LAGS = (0, 1, 2, 3, 4, 6, 7, 8, 9, 10)
 
 
 def flipped(index, mask):
@@ -107,20 +108,21 @@
         ).astype(jnp.bfloat16)
 
     def tile(j, side):
-        rows_in = theirs[side, part(j)]
+        span = pl.ds(pl.multiple_of(j * TILE, TILE), TILE)
+        rows_in = theirs[side, span]
         which = first ^ side
 
         def block(i, acc):
             lines = pl.ds(pl.multiple_of(i * ROWS, ROWS), ROWS)
             mine = p_ref[lines]
             gram = lax.dot_general(mine, rows_in, (((1,), (1,)), ((), ())), preferred_element_type=jnp.float32)
-            residual = gram * inverse - o_ref[which, lines, part(j)].astype(jnp.float32)
+            residual = gram * inverse - o_ref[which, lines, span].astype(jnp.float32)
             weight = ((STUDENT_NU + 1.0) * residual / (STUDENT_NU + residual * residual)).astype(jnp.bfloat16)
-            weights[side, lines, part(j)] = weight
+            weights[side, lines, span] = weight
             return acc + lax.dot_general(weight, mine, (((0,), (0,)), ((), ())), preferred_element_type=jnp.float32)
 
-        acc = lax.fori_loop(0, rows // ROWS, block, jnp.zeros((CHUNK, samples), jnp.float32))
-        answers[side, part(j)] = (acc * inverse).astype(jnp.bfloat16)
+        acc = lax.fori_loop(0, rows // ROWS, block, jnp.zeros((TILE, samples), jnp.float32))
+        answers[side, span] = (acc * inverse).astype(jnp.bfloat16)
 
     def level_step(k):
         def run(j):
@@ -131,28 +133,24 @@
 
         return run
 
-    def tile_steps(t, lag_near, lag_far):
-        @pl.loop(0, 2)
-        def _(side):
-            j = t - lag_near - side * (lag_far - lag_near)
-
-            @pl.when((j >= 0) & (j < count))
-            def _():
-                @pl.when(side == 0)
-                def _():
-                    if direct:
-                        go_near(j).wait_recv()
-                        go_far(j).start()
-
-                @pl.when(side == 1)
-                def _():
-                    go_far(j).wait_recv()
-
-                tile(j, side)
-
-                @pl.when(side == 1)
-                def _():
-                    go_back(j).start()
+    def near_step(j):
+        if direct:
+            go_near(j).wait_recv()
+            go_far(j).start()
+
+    def far_step(j):
+        go_far(j).wait_recv()
+
+    per_tile = TILE // CHUNK
+
+    def tile_step(turn):
+        side = turn % 2
+        tile(turn // 2, side)
+
+        @pl.when(side == 1)
+        def _():
+            for k in range(per_tile):
+                go_back(turn // 2 * per_tile + k).start()
 
     def back_step(j):
         go_back(j).wait_recv()
@@ -179,33 +177,35 @@
         return run
 
     def own_step(j):
-        own[part(j)] = jnp.dot(weights[0, part(j)], theirs[0], preferred_element_type=jnp.float32) + jnp.dot(
-            weights[1, part(j)], theirs[1], preferred_element_type=jnp.float32
+        lines = pl.ds(pl.multiple_of(j * ROWS, ROWS), ROWS)
+        own[lines] = jnp.dot(weights[0, lines], theirs[0], preferred_element_type=jnp.float32) + jnp.dot(
+            weights[1, lines], theirs[1], preferred_element_type=jnp.float32
         )
 
-    steps = [level_step(k) for k in range(depth)] + ["near", "far", back_step]
+    steps = [level_step(k) for k in range(depth)] + [near_step, far_step, back_step]
     steps += [home_step] if direct else [None]
     steps += [return_step(k) for k in range(depth)]
     when = list(lags[: len(steps)])
-    own_lag = when[depth + 1] + count
+    tile_lag = when[depth] + TILE // CHUNK - 1
+    own_lag = tile_lag + 2 * (rows // TILE)
     assert all(a is not None for a in when)
 
-    @pl.loop(0, count + max(max(when), own_lag))
+    @pl.loop(0, max(count + max(when), own_lag + rows // ROWS))
     def _(t):
         for step, lag in zip(steps, when):
-            if step == "near":
-                tile_steps(t, lag, when[depth + 1])
-            elif step not in (None, "far"):
+            if step is not None:
 
                 @pl.when((t >= lag) & (t < lag + count))
                 def _(step=step, lag=lag):
                     step(t - lag)
 
-        @pl.when(t >= own_lag)
+        @pl.when((t >= tile_lag) & (t < tile_lag + 2 * (rows // TILE)))
         def _():
-            @pl.when(t < own_lag + count)
-            def _():
-                own_step(t - own_lag)
+            tile_step(t - tile_lag)
+
+        @pl.when((t >= own_lag) & (t < own_lag + rows // ROWS))
+        def _():
+            own_step(t - own_lag)
 
     last = returned[depth]
     adjoint_ref[...] = (own[...] * inverse + last[...].astype(jnp.float32)).astype(jnp.bfloat16)

time: 144 us -> 150 us (1.042); the launches traced: 146 us -> 148 us
    pallas_call x1, Pallas kernels: 121 us -> 125 us  [tile_call(): pl.pallas_call(functools.partial(tile_kernel, direct, spec), out_shape=ja...]
    pallas_call x1, Pallas kernels: 21 us -> 18.3 us  [sum_call(): pl.pallas_call(sum_kernel, out_shape=jax.ShapeDtypeStruct((2, samples), j...]
where the time goes in v2:
time: 150 us; the launch traced here: 148 us
  Pallas kernels  143 us (95%)
  between operations  1.99 us (1%)
  local copies, waits for them, and re-layouts  1.78 us (1%)
    pallas_call x1, Pallas kernels, tile_call(): pl.pallas_call(functools.partial(tile_kernel, direct, spec), out_shape=ja...  125 us
    pallas_call x1, Pallas kernels, sum_call(): pl.pallas_call(sum_kernel, out_shape=jax.ShapeDtypeStruct((2, samples), j...  18.3 us

profile of v2, /device:TPU:2, one launch (start us, length us, event | category | flops | bytes accessed | tf_op | source)
XLA Modules:
  0.0 147.8 jit_solution(6369034599238763862)
XLA Ops:
  0.0 1.2 slice.3
  3.1 0.1 pad_add_fusion
  3.2 0.0 copy-start
  3.2 0.0 copy-start.1
  3.2 125.7 %conditional.1 = (bf16[1024,384]{1,0:T(8,128)(2,1)S(1)}) conditional(s32[]{:T(128)} %clamp.3, (s32[4]{0:T(128)S(1)}, bf16[1024,384]{1,0:T(8,128)(2,1)}, bf16[2,1024,1024]{2,1,0:T(8,128)(2,1)}) %tuple.53, (s32[4]{0:T(128)S(1)}, bf16[1024,384]{1,0:T(8,128)(2,1)}, bf16[2,1024,1024]{2,1,0:T(8,128)(2,1)}) %tuple.53, ...), branch_computations={%region_0.1_spmd, %region_1.2_spmd, %region_2.3_spmd, %region_3.4_... | conditional | bytes 8 | solution.py:409
  3.4 125.2 %tiles_6.1 = bf16[1024,384]{1,0:T(8,128)(2,1)S(1)} custom-call(s32[4]{0:T(128)S(1)} %get-tuple-element.142.flag_ref, bf16[1024,384]{1,0:T(8,128)(2,1)} %get-tuple-element.143.p_ref, bf16[2,1024,1024]{2,1,0:T(8,128)(2,1)} %get-tuple-element.144.o_hbm), custom_call_target="tpu_custom_call" | custom-call | tf_op jit(solution)/shard_map/cond/branch_8_fun/tiles_6/pallas_call | solution.py:229
  129.0 0.0 copy-done
  129.0 0.0 copy-done.1
  129.0 18.3 %sum_cells.1 = f32[2,384]{1,0:T(2,128)S(1)} custom-call(bf16[1024,384]{1,0:T(8,128)(2,1)S(1)} %get-tuple-element.166.adjoint_ref, bf16[1024,512]{1,0:T(8,128)(2,1)S(1)} %copy-done, bf16[512,512]{1,0:T(8,128)(2,1)S(1)} %copy-done.1), custom_call_target="tpu_custom_call" | custom-call | tf_op jit(solution)/shard_map/sum_cells/pallas_call | solution.py:345
  147.3 0.6 copy.23
Async XLA Ops:
  3.2 125.7 %copy-start = (bf16[1024,512]{1,0:T(8,128)(2,1)S(1)}, bf16[1024,512]{1,0:T(8,128)(2,1)}, u32[]{:S(2)}) copy-start(bf16[1024,512]{1,0:T(8,128)(2,1)} %g_ref.1) | copy-start | bytes 3145732
  3.2 125.7 %copy-start.1 = (bf16[512,512]{1,0:T(8,128)(2,1)S(1)}, bf16[512,512]{1,0:T(8,128)(2,1)}, u32[]{:S(2)}) copy-start(bf16[512,512]{1,0:T(8,128)(2,1)} %constant.22.clone.order_ref) | copy-start | bytes 1572868
